TPU v7x, 128 devices: a whole 4x4x4 slice. The times are simulated.
128 devices in a mesh: inst: 8 (over y_lo, z), space: 16 (over x, y_hi, core).
Axes of the slice: x: 4, y: 4 (y_hi: 2, y_lo: 2; y = y_hi * 2 + y_lo), z: 4, core: 2. Of those that a mesh axis runs over, the one named last changes fastest.
Arguments:
- velocity: float32 [16, 3, 16, 256, 256], P('inst', None, 'space'), may hold values from -6 to 6
- frequency: float32 [1], replicated, may hold values from 0.6 to 1.4
- slot_time: int32 [16], replicated, may hold values from 0 to 15, each once
- mirror_rows: int32 [256], replicated, may hold values from 0 to 255, as said below
Outputs:
- orbit: float32 [16, 3, 16, 256, 256], P('inst', None, 'space')
- defect: float32 [16, 3, 16, 256, 256], P('inst', None, 'space')
- frequency_new: float32 [1], replicated
Inputs may be any that keep to these rules, and one draw needn't show every extreme that they name: `slot_time`: a permutation; slot s lies on index s // 2 of inst. mirror_rows[z] = (256 + c - z) mod 256 for one whole number c of the draw.
All inputs are finite; a program needn't handle non-finite values.
Results may differ from a plain program's by a relative error of at most 0.0001.
Values sent between devices are 32-bit elements; how exact they have to be, the bound alone decides.
A program may use at most 128 MiB of HBM per device.

v0:
```python
import jax
import jax.numpy as jnp
from jax import lax
from jax.sharding import PartitionSpec as P

ITERS = 2


viscosity = 0.5
descent_step = 0.001
frequency_rate = 0.025


def extended(array, sides, width):
    for axis, dim in sides:
        size, length = (lax.axis_size(axis), array.shape[dim])
        up = [(i, (i + 1) % size) for i in range(size - 1)]
        down = [(j, i) for i, j in up]
        last = lax.slice_in_dim(array, length - width, length, axis=dim)
        leading = lax.slice_in_dim(array, 0, width, axis=dim)
        before = lax.ppermute(last, axis, up)
        after = lax.ppermute(leading, axis, down)
        array = jnp.concatenate([before, array, after], axis=dim)
    return array


def spectral_weights(later, earlier, total):
    gap = (later[:, None] - earlier[None, :]) % total
    angle = jnp.pi * gap.astype(jnp.float32) / total
    parity = 1.0 - 2.0 * (gap % 2).astype(jnp.float32)
    nonzero = gap != 0
    sine = jnp.where(nonzero, jnp.sin(angle), 1.0)
    return jnp.where(nonzero, 0.5 * parity * jnp.cos(angle) / sine, 0.0)


def partner_rows(later, earlier, total):
    return ((later[:, None] + total // 2) % total == earlier[None, :]).astype(jnp.float32)


def reflect_halves(halves, mirror):
    flipped = jnp.take(jnp.flip(halves, axis=-3), mirror, axis=-1)
    sign = jnp.array([1.0, 1.0, -1.0], dtype=halves.dtype).reshape(3, 1, 1, 1, 1)
    return flipped * sign


def reflect(field, mirror):
    shape = field.shape
    halves = field.reshape(shape[:-2] + (2, shape[-2] // 2, shape[-1]))
    return reflect_halves(halves, mirror).reshape(shape)


def spatial_terms(padded, speed):
    center = padded[:, :, 1:-1]
    laplace = (
        padded[:, :, 2:]
        + padded[:, :, :-2]
        + jnp.roll(center, 1, axis=3)
        + jnp.roll(center, -1, axis=3)
        + jnp.roll(center, 1, axis=4)
        + jnp.roll(center, -1, axis=4)
        - 6.0 * center
    )
    slope = 0.5 * (jnp.roll(center, -1, axis=3) - jnp.roll(center, 1, axis=3))
    return (laplace, speed * slope)


def apply_time(matrix, field):
    flat = field.reshape(field.shape[0], -1)
    mixed = jnp.dot(matrix, flat, precision=lax.Precision.HIGHEST)
    return mixed.reshape((matrix.shape[0],) + field.shape[1:])


def twice_weights(later, earlier, total):
    every = jnp.arange(total)
    left = spectral_weights(later, every, total)
    right = spectral_weights(every, earlier, total)
    return jnp.dot(left, right, precision=lax.Precision.HIGHEST)


def shards(velocity, frequency, slot_time, mirror_rows):
    slots, components, planes, width_x, width_z = velocity.shape
    total = slot_time.shape[0]
    window = planes * lax.axis_size("space")
    plane_ids = (lax.axis_index("space") * planes + jnp.arange(planes)).astype(jnp.float32)
    speed_inner = (2.0 * (plane_ids + 0.5) / window - 1.0).reshape(planes, 1, 1)
    own_times = lax.dynamic_slice_in_dim(slot_time, lax.axis_index("inst") * slots, slots)
    entries = total * components * window * width_x * width_z
    omega = frequency[0]
    field = velocity
    defect = velocity
    for step in range(ITERS):
        matrix = jnp.concatenate(
            [
                spectral_weights(own_times, slot_time, total),
                spectral_weights(own_times + total // 2, slot_time, total),
                partner_rows(own_times, slot_time, total),
                twice_weights(own_times, slot_time, total),
                twice_weights(own_times + total // 2, slot_time, total),
            ],
            axis=0,
        )
        combined = apply_time(matrix, lax.all_gather(field, "inst", axis=0, tiled=True))
        symmetric = 0.5 * (field + reflect(combined[2 * slots : 3 * slots], mirror_rows))
        derivative = 0.5 * (combined[:slots] + reflect(combined[slots : 2 * slots], mirror_rows))
        second = 0.5 * (
            combined[3 * slots : 4 * slots] + reflect(combined[4 * slots :], mirror_rows)
        )
        stacked = jnp.concatenate([symmetric, derivative], axis=1)
        padded = extended(stacked, (("space", 2),), 1)
        laplace, advect = spatial_terms(padded[:, :3], speed_inner)
        defect = omega * derivative - viscosity * laplace + advect
        rate_lap, rate_adv = spatial_terms(padded[:, 3:], speed_inner)
        defect_rate = omega * second - viscosity * rate_lap + rate_adv
        defect_wide = extended(defect, (("space", 2),), 1)
        laplace, advect = spatial_terms(defect_wide, speed_inner)
        drift = lax.psum(jnp.sum(defect * derivative), ("inst", "space"))
        field = symmetric + descent_step * (omega * defect_rate + viscosity * laplace + advect)
        omega = omega - frequency_rate * drift / entries
    return (field, defect, jnp.reshape(omega, (1,)))


def solution(mesh):
    in_specs = (P("inst", None, "space", None, None), P(), P(), P())
    out_specs = (P("inst", None, "space", None, None), P("inst", None, "space", None, None), P())
    return jax.shard_map(shards, mesh=mesh, in_specs=in_specs, out_specs=out_specs, check_vma=False)
```

profile of v0, /device:TPU:1, one launch (start us, length us, event | category | flops | bytes accessed | tf_op | source)
XLA Modules:
  0.0 865.9 jit_solution(6998115297838348338)
XLA Ops:
  8.9 135.5 %all-gather.3.cloned.1.call-done = f32[16,3,1,256,256]{4,3,2,1,0:T(8,128)} async-done(((f32[2,3,1,256,256]{4,3,2,1,0:T(8,128)}), f32[16,3,1,256,256]{4,3,2,1,0:T(8,128)}) %all-gather.3.cloned.1.call-update) | async-done | bytes 12582928 | tf_op jit(solution)/shard_map/all_gather | solution.py:102
  144.3 16.4 %copy.80 = f32[2,8,768,256]{3,1,2,0:T(8,128)} copy(f32[2,8,768,256]{3,2,1,0:T(8,128)} %bitcast.121) | data formatting | bytes 25165824
  160.7 13.4 %fusion.195 = f32[10,196608]{1,0:T(8,128)S(1)} fusion(f32[10,16]{1,0:T(8,128)S(1)} %concatenate.196, f32[16,196608]{1,0:T(8,128)} %bitcast.115), kind=kOutput, calls=%fused_computation.268 | convolution fusion | flops 377487360 | bytes 20447872 | tf_op jit(solution)/shard_map/dot_general | solution.py:69
  174.1 4.0 fusion.170
  179.1 5.8 rev.19
  184.9 2.9 gather_fusion
  192.7 8.6 rev.20
  201.3 4.0 gather_fusion.1
  205.2 2.5 copy.68
  207.7 2.7 copy.85
  210.4 3.6 copy.69
  214.1 9.2 %rev.21 = f32[2,3,1,2,128,256]{4,3,5,1,0,2:T(2,128)} reverse(f32[2,3,1,2,128,256]{4,3,5,1,0,2:T(2,128)} %copy.69), dimensions={3} | reverse | bytes 3145728 | tf_op jit(solution)/shard_map/jit(_flip)/rev | solution.py:41
  223.3 5.4 gather_fusion.2
  228.7 3.6 copy.70
  239.6 2.6 collective-permute-start
  242.2 4.4 collective-permute-start.1
  249.0 30.9 %collective-permute-done = f32[2,6,1,256,256]{4,3,1,0,2:T(8,128)} collective-permute-done((f32[2,6,1,256,256]{4,3,1,0,2:T(8,128)}, f32[2,6,1,256,256]{4,3,1,0,2:T(8,128)}, u32[]{:S(2)}, u32[]{:S(2)}) %collective-permute-start) | collective-permute-done | bytes 3145760 | tf_op jit(solution)/shard_map/ppermute | solution.py:22
  280.0 50.5 %collective-permute-done.1 = f32[2,6,1,256,256]{4,3,1,0,2:T(8,128)} collective-permute-done((f32[2,6,1,256,256]{4,3,1,0,2:T(8,128)}, f32[2,6,1,256,256]{4,3,1,0,2:T(8,128)}, u32[]{:S(2)}, u32[]{:S(2)}) %collective-permute-start.1) | collective-permute-done | bytes 3145760 | tf_op jit(solution)/shard_map/ppermute | solution.py:21
  330.5 3.8 multiply_reduce_fusion.1
  336.2 5.9 collective-permute-start.3
  343.9 14.3 %collective-permute-done.2 = f32[2,3,1,256,256]{4,3,1,0,2:T(8,128)S(1)} collective-permute-done((f32[2,3,1,256,256]{4,3,1,0,2:T(8,128)S(1)}, f32[2,3,1,256,256]{4,3,1,0,2:T(8,128)S(1)}, u32[]{:S(2)}, u32[]{:S(2)}) %collective-permute-start.2) | collective-permute-done | bytes 1572896 | tf_op jit(solution)/shard_map/ppermute | solution.py:22
  360.7 5.9 fusion.42
  366.6 144.4 %all-gather.5.cloned.1.call-done = f32[16,3,1,256,256]{4,3,2,1,0:T(8,128)} async-done(((f32[2,3,1,256,256]{4,3,2,1,0:T(8,128)}), f32[16,3,1,256,256]{4,3,2,1,0:T(8,128)}) %all-gather.5.cloned.1.call-update) | async-done | bytes 12582928 | tf_op jit(solution)/shard_map/all_gather | solution.py:102
  511.0 16.4 %copy.86 = f32[2,8,768,256]{3,1,2,0:T(8,128)} copy(f32[2,8,768,256]{3,2,1,0:T(8,128)} %bitcast.122) | data formatting | bytes 25165824
  527.4 13.4 %fusion.196 = f32[10,196608]{1,0:T(8,128)S(1)} fusion(f32[10,16]{1,0:T(8,128)S(1)} %concatenate.196, f32[16,196608]{1,0:T(8,128)} %bitcast.114), kind=kOutput, calls=%fused_computation.269 | convolution fusion | flops 377487360 | bytes 20447872 | tf_op jit(solution)/shard_map/dot_general | solution.py:69
  540.8 4.0 fusion.169
  545.8 5.8 rev.22
  551.6 2.9 gather_fusion.3
  557.3 2.1 copy.76
  559.4 8.6 rev.24
  568.0 4.0 gather_fusion.5
  571.9 2.5 copy.77
  574.4 2.7 copy.89
  577.1 3.6 copy.74
  580.8 9.1 %rev.23 = f32[2,3,1,2,128,256]{4,3,5,1,0,2:T(2,128)} reverse(f32[2,3,1,2,128,256]{4,3,5,1,0,2:T(2,128)} %copy.74), dimensions={3} | reverse | bytes 3145728 | tf_op jit(solution)/shard_map/jit(_flip)/rev | solution.py:41
  589.8 5.4 gather_fusion.4
  595.2 3.6 copy.75
  607.2 2.6 collective-permute-start.4
  609.9 4.4 collective-permute-start.5
  614.3 121.5 %psum.14 = f32[]{:T(128)} all-reduce(f32[]{:T(128)} %get-tuple-element.15), channel_id=1, replica_groups=mesh['inst'=8,'space'=16] {'inst','space'}, use_global_device_ids=true, to_apply=%region_1.3 | all-reduce | flops 1 | bytes 8 | tf_op jit(solution)/shard_map/psum | solution.py:116
  742.4 4.6 multiply_reduce_fusion
  747.0 2.5 collective-permute-start.6
  749.6 4.5 collective-permute-start.7
  755.4 2.2 fusion.181
  757.6 83.9 %psum.15 = f32[]{:T(128)} all-reduce(f32[]{:T(128)} %get-tuple-element.13), channel_id=1, replica_groups=mesh['inst'=8,'space'=16] {'inst','space'}, use_global_device_ids=true, to_apply=%region_3.5 | all-reduce | flops 1 | bytes 8 | tf_op jit(solution)/shard_map/psum | solution.py:116
  844.7 2.3 fusion.174
  847.0 2.9 fusion.175
  851.4 6.0 fusion.21
  (119 shorter events, 45.8 us)
Async XLA Ops:
  7.2 0.8 copy-start.26
  7.2 1.7 copy-start.28
  7.2 137.1 %all-gather.3.cloned.1.call-start = ((), (), s32[]{:S(2)}) async-start(), calls=%async_computation | async-start | bytes 14155776 | tf_op jit(solution)/shard_map/all_gather | solution.py:102
  7.9 503.1 %all-gather.5.cloned.1.call-start = ((), (), s32[]{:S(2)}) async-start(), calls=%async_computation.1 | async-start | bytes 14155776 | tf_op jit(solution)/shard_map/all_gather | solution.py:102
  232.3 1.9 copy-start.12
  232.3 1.9 copy-start.27
  234.2 1.6 copy-start.6
  235.8 1.7 copy-start.4
  239.6 40.4 %collective-permute-start = (f32[2,6,1,256,256]{4,3,1,0,2:T(8,128)}, f32[2,6,1,256,256]{4,3,1,0,2:T(8,128)}, u32[]{:S(2)}, u32[]{:S(2)}) collective-permute-start(f32[2,6,1,256,256]{4,3,1,0,2:T(8,128)} %pad_maximum_fusion), channel_id=1, source_target_pairs={{1,0},{2,1},{3,2},{4,3},{5,4},{6,5},{7,6},{8,7},{9,8},{10,9},{11,1... | collective-permute-start | bytes 9437192 | tf_op jit(solution)/shard_map/ppermute | solution.py:22
  242.2 88.3 %collective-permute-start.1 = (f32[2,6,1,256,256]{4,3,1,0,2:T(8,128)}, f32[2,6,1,256,256]{4,3,1,0,2:T(8,128)}, u32[]{:S(2)}, u32[]{:S(2)}) collective-permute-start(f32[2,6,1,256,256]{4,3,1,0,2:T(8,128)} %pad_maximum_fusion), channel_id=1, source_target_pairs={{0,1},{1,2},{2,3},{3,4},{4,5},{5,6},{6,7},{7,8},{8,9},{9,10},{10,1... | collective-permute-start | bytes 9437192 | tf_op jit(solution)/shard_map/ppermute | solution.py:21
  248.7 81.7 %copy-start.5 = (f32[2,3,1,2,128,256]{5,4,3,2,1,0:T(8,128)S(1)}, f32[2,3,1,2,128,256]{5,4,3,2,1,0:T(8,128)}, u32[]{:S(2)}) copy-start(f32[2,3,1,2,128,256]{5,4,3,2,1,0:T(8,128)} %copy-done.4) | copy-start | bytes 4718596
  248.7 81.7 %copy-start.7 = (f32[2,3,1,256,256]{4,3,2,1,0:T(8,128)S(1)}, f32[2,3,1,256,256]{4,3,2,1,0:T(8,128)}, u32[]{:S(2)}) copy-start(f32[2,3,1,256,256]{4,3,2,1,0:T(8,128)} %param.12) | copy-start | bytes 4718596
  248.7 81.7 %copy-start.10 = (f32[2,3,1,256,256]{4,3,1,0,2:T(8,128)S(1)}, f32[2,3,1,256,256]{4,3,1,0,2:T(8,128)}, u32[]{:S(2)}) copy-start(f32[2,3,1,256,256]{4,3,1,0,2:T(8,128)} %get-tuple-element.20) | copy-start | bytes 4718596
  330.5 11.6 %copy-start.15 = (f32[2,196608]{1,0:T(2,128)S(1)}, f32[2,196608]{1,0:T(2,128)}, u32[]{:S(2)}) copy-start(f32[2,196608]{1,0:T(2,128)} %get-tuple-element.31) | copy-start | bytes 4718596
  334.3 24.0 %collective-permute-start.2 = (f32[2,3,1,256,256]{4,3,1,0,2:T(8,128)S(1)}, f32[2,3,1,256,256]{4,3,1,0,2:T(8,128)S(1)}, u32[]{:S(2)}, u32[]{:S(2)}) collective-permute-start(f32[2,3,1,256,256]{4,3,1,0,2:T(8,128)S(1)} %get-tuple-element.16), channel_id=1, source_target_pairs={{1,0},{2,1},{3,2},{4,3},{5,4},{6,5},{7,6},{8,7},{9,8},{10,9},{11,1... | collective-permute-start | bytes 4718600 | tf_op jit(solution)/shard_map/ppermute | solution.py:22
  336.2 23.2 %collective-permute-start.3 = (f32[2,3,1,256,256]{4,3,1,0,2:T(8,128)S(1)}, f32[2,3,1,256,256]{4,3,1,0,2:T(8,128)S(1)}, u32[]{:S(2)}, u32[]{:S(2)}) collective-permute-start(f32[2,3,1,256,256]{4,3,1,0,2:T(8,128)S(1)} %get-tuple-element.16), channel_id=1, source_target_pairs={{0,1},{1,2},{2,3},{3,4},{4,5},{5,6},{6,7},{7,8},{8,9},{9,10},{10,1... | collective-permute-start | bytes 4718600 | tf_op jit(solution)/shard_map/ppermute | solution.py:21
  343.4 17.3 %copy-start.14 = (f32[2,3,1,2,128,256]{5,4,3,2,1,0:T(8,128)S(1)}, f32[2,3,1,2,128,256]{5,4,3,2,1,0:T(8,128)}, u32[]{:S(2)}) copy-start(f32[2,3,1,2,128,256]{5,4,3,2,1,0:T(8,128)} %get-tuple-element.84) | copy-start | bytes 4718596
  358.2 1.2 copy-start.24
  359.4 1.2 copy-start.25
  598.8 1.9 copy-start.11
  600.7 1.8 copy-start
  602.5 1.2 copy-start.2
  607.2 133.6 %collective-permute-start.4 = (f32[2,6,1,256,256]{4,3,1,0,2:T(8,128)}, f32[2,6,1,256,256]{4,3,1,0,2:T(8,128)}, u32[]{:S(2)}, u32[]{:S(2)}) collective-permute-start(f32[2,6,1,256,256]{4,3,1,0,2:T(8,128)} %pad_maximum_fusion.1), channel_id=1, source_target_pairs={{1,0},{2,1},{3,2},{4,3},{5,4},{6,5},{7,6},{8,7},{9,8},{10,9},{11,1... | collective-permute-start | bytes 9437192 | tf_op jit(solution)/shard_map/ppermute | solution.py:22
  609.9 131.0 %collective-permute-start.5 = (f32[2,6,1,256,256]{4,3,1,0,2:T(8,128)}, f32[2,6,1,256,256]{4,3,1,0,2:T(8,128)}, u32[]{:S(2)}, u32[]{:S(2)}) collective-permute-start(f32[2,6,1,256,256]{4,3,1,0,2:T(8,128)} %pad_maximum_fusion.1), channel_id=1, source_target_pairs={{0,1},{1,2},{2,3},{3,4},{4,5},{5,6},{6,7},{7,8},{8,9},{9,10},{10,1... | collective-permute-start | bytes 9437192 | tf_op jit(solution)/shard_map/ppermute | solution.py:21
  738.9 1.9 copy-start.1
  738.9 3.0 copy-start.3
  739.0 3.5 copy-start.8
  742.4 11.7 %copy-start.16 = (f32[2,196608]{1,0:T(2,128)S(1)}, f32[2,196608]{1,0:T(2,128)}, u32[]{:S(2)}) copy-start(f32[2,196608]{1,0:T(2,128)} %get-tuple-element.26) | copy-start | bytes 4718596
  747.0 102.9 %collective-permute-start.6 = (f32[2,3,1,256,256]{4,3,1,0,2:T(8,128)}, f32[2,3,1,256,256]{4,3,1,0,2:T(8,128)}, u32[]{:S(2)}, u32[]{:S(2)}) collective-permute-start(f32[2,3,1,256,256]{4,3,1,0,2:T(8,128)} %get-tuple-element.14), channel_id=1, source_target_pairs={{1,0},{2,1},{3,2},{4,3},{5,4},{6,5},{7,6},{8,7},{9,8},{10,9},{11,1... | collective-permute-start | bytes 4718600 | tf_op jit(solution)/shard_map/ppermute | solution.py:22
  749.6 100.4 %collective-permute-start.7 = (f32[2,3,1,256,256]{4,3,1,0,2:T(8,128)}, f32[2,3,1,256,256]{4,3,1,0,2:T(8,128)}, u32[]{:S(2)}, u32[]{:S(2)}) collective-permute-start(f32[2,3,1,256,256]{4,3,1,0,2:T(8,128)} %get-tuple-element.14), channel_id=1, source_target_pairs={{0,1},{1,2},{2,3},{3,4},{4,5},{5,6},{6,7},{7,8},{8,9},{9,10},{10,1... | collective-permute-start | bytes 4718600 | tf_op jit(solution)/shard_map/ppermute | solution.py:21
  844.7 5.3 copy-start.19
  844.7 5.3 copy-start.20
  844.7 5.3 copy-start.21
  844.7 5.3 copy-start.22
  844.7 5.3 copy-start.23
  847.0 3.1 copy-start.9
  847.0 3.5 copy-start.13
  847.0 4.0 copy-start.17
  847.0 4.4 copy-start.18
Sparse Core Ops, SparseCore 0:
  9.7 134.6 all-gather.2
  366.7 144.2 all-gather.4
where the time goes:
time: 874 us; the launch traced here: 866 us
  waiting for transfers between devices  377 us (43%)
  blocking collectives  205 us (23%)
  local copies, waits for them, and re-layouts  177 us (20%)
  other arithmetic  31.6 us (4%)
  starting transfers between devices  29.1 us (3%)
  matrix products  27.2 us (3%)
  between operations  18.2 us (2%)
    all_gather x2, waiting for transfers between devices, shards(): lax.all_gather(field, 'inst', axis=0, tiled=True)  280 us
    psum x2, blocking collectives, shards(): drift = lax.psum(jnp.sum(defect * derivative), ('inst', 'space'))  205 us
    unnamed x70, local copies, waits for them, and re-layouts  51.8 us
    ppermute x4, waiting for transfers between devices, extended(): before = lax.ppermute(last, axis, up)  51.7 us
    rev x6, local copies, waits for them, and re-layouts, reflect_halves(): flipped = jnp.take(jnp.flip(halves, axis=-3), mirror, axis=-1)  47.2 us
    ppermute x4, waiting for transfers between devices, extended(): after = lax.ppermute(leading, axis, down)  45.3 us
    gather x12, local copies, waits for them, and re-layouts, reflect_halves(): flipped = jnp.take(jnp.flip(halves, axis=-3), mirror, axis=-1)  39.1 us
    dot_general x2, matrix products, apply_time(): mixed = jnp.dot(matrix, flat, precision=lax.Precision.HIGHEST)  26.7 us
  transfers between devices with their start and end apart: 10, of which 6 were waited for; matrix products, arithmetic and copies ran while one was open for 2% of the time, Pallas kernels for 0%

commit v1 on v0

v1 whole, which is shorter than its diff:
```python
import functools
import math

import jax
import jax.numpy as jnp
from jax import lax
from jax.experimental import pallas as pl
from jax.experimental.pallas import tpu as pltpu
from jax.sharding import PartitionSpec as P

VISCOSITY = 0.5
DESCENT = 0.001
FREQUENCY_RATE = 0.025
MESH = pl.DeviceIdType.MESH
F32 = jnp.float32


def device(x, y, z, core):
    return ((y % 2) * 4 + z, x * 4 + (y // 2) * 2 + core)


def chip_of(j):
    y = j // 4
    r = j % 4
    return y, jnp.where(y % 2 == 0, r, 3 - r)


def weight(k):
    k = k % 16
    if k == 0:
        return 0.0
    angle = math.pi * k / 16
    return 0.5 * (-1.0) ** k * math.cos(angle) / math.sin(angle)


def kernel(
    freq, times, mirror, vel, orbit, defect, fout,
    rbuf0, rbuf1, rbuf2, fld, orb, xsend, xrecv, obuf, mbuf, dbuf, mat, kmat, acc, drift, inv,
    in_send, in_recv, x_send, x_recv, y_send, y_recv, o_send, o_recv, d_send, d_recv,
):
    inst = lax.axis_index("inst")
    space = lax.axis_index("space")
    z = inst % 4
    yhi = space // 2 % 2
    y = yhi * 2 + inst // 4
    x = space // 4
    core = space % 2
    myj = y * 4 + jnp.where(y % 2 == 0, z, 3 - z)
    outs = (defect, orbit)
    rbuf = (rbuf0, rbuf1, rbuf2)

    barrier = pltpu.get_barrier_semaphore()
    place = myj * 2 + core

    def greet_chip(k, carry):
        d = (k + place) % 32
        cy, cz = chip_of(d // 2)
        pl.semaphore_signal(
            barrier, inc=1, device_id=device(x, cy, cz, d % 2), device_id_type=MESH
        )
        return carry

    lax.fori_loop(1, 32, greet_chip, 0)
    for k in range(1, 4):
        pl.semaphore_signal(
            barrier, inc=1, device_id=device((x + k) % 4, y, z, core), device_id_type=MESH
        )
    far = device((x + jnp.where(core == 1, 1, 3)) % 4, y, z, 1 - core)
    near = device(x, y, z, 1 - core)
    pl.semaphore_signal(barrier, inc=1, device_id=far, device_id_type=MESH)

    mat[...] = (
        lax.broadcasted_iota(jnp.int32, (256, 256), 0) == mirror[...]
    ).astype(F32).astype(jnp.bfloat16)
    rows = lax.broadcasted_iota(jnp.int32, (128, 128), 0)
    cols = lax.broadcasted_iota(jnp.int32, (128, 128), 1)
    gap = (rows // 8 - cols // 8 + 16) % 16
    table = jnp.zeros((128, 128), F32)
    for k in range(1, 16):
        table = jnp.where(gap == k, jnp.float32(weight(k)), table)
    kmat[...] = jnp.where(rows % 8 == cols % 8, table, 0.0)

    def invert(t, carry):
        def find(s, found):
            return jnp.where(times[s] == t, s, found)

        inv[t] = lax.fori_loop(0, 16, find, jnp.int32(0))
        return carry

    lax.fori_loop(0, 16, invert, 0)
    bottom = (x == 0) & (core == 0)
    top = (x == 3) & (core == 1)

    @pl.when(bottom)
    def _():
        fld[:, 0] = jnp.zeros((4, 3, 128, 256), F32)

    @pl.when(top)
    def _():
        fld[:, 3] = jnp.zeros((4, 3, 128, 256), F32)

    pl.semaphore_wait(barrier, 35)

    def send_in(c):
        def body(k, carry):
            j = (k + myj) % 16
            cy, cz = chip_of(j)
            di, ds = device(x, cy, cz, yhi)
            src = vel.at[:, c, :, j]
            dst = rbuf[c].at[core, pl.ds(2 * inst, 2)]
            mine = (di == inst) & (ds == space)

            @pl.when(mine)
            def _():
                pltpu.make_async_copy(src, dst, in_recv.at[c]).start()

            @pl.when(jnp.logical_not(mine))
            def _():
                pltpu.make_async_remote_copy(
                    src, dst, in_send, in_recv.at[c], device_id=(di, ds), device_id_type=MESH
                ).start()

            return carry

        lax.fori_loop(0, 16, body, 0)

    for c in range(3):
        send_in(c)

    def reflect_z(v):
        high = v.astype(jnp.bfloat16)
        rest = v - high.astype(F32)
        middle = rest.astype(jnp.bfloat16)
        low = (rest - middle.astype(F32)).astype(jnp.bfloat16)
        m = mat[...]
        parts = [jnp.dot(u, m, preferred_element_type=F32) for u in (high, middle, low)]
        return parts[0] + (parts[1] + parts[2])

    def signed(c, v):
        return -v if c == 2 else v

    left = chip_of((myj + 15) % 16)
    right = chip_of((myj + 1) % 16)

    def send_halo(k, c):
        for p in range(2):
            part = pl.ds(16 * p, 16)
            tiles = fld[k, 1 + p, c].reshape(16, 8, 256)
            xsend[k, 0, c, part] = tiles[:, 0]
            xsend[k, 1, c, part] = tiles[:, 7]
        for side, wraps in ((0, myj == 0), (1, myj == 15)):

            @pl.when(wraps)
            def _():
                turned = signed(c, reflect_z(xsend[k, side, c]))
                for p in range(2):
                    xsend[k, side, c, pl.ds(16 * p, 8)] = turned[16 * p + 8 : 16 * p + 16]
                    xsend[k, side, c, pl.ds(16 * p + 8, 8)] = turned[16 * p : 16 * p + 8]

        for side, (cy, cz) in ((0, left), (1, right)):
            pltpu.make_async_remote_copy(
                xsend.at[k, side, c], xrecv.at[k, 1 - side, c], x_send,
                x_recv.at[k, 1 - side, c], device_id=device(x, cy, cz, core), device_id_type=MESH,
            ).start()

        def planes(up, target):
            src, dst = (2, 0) if up else (1, 3)
            pltpu.make_async_remote_copy(
                fld.at[k, src, c], fld.at[k, dst, c], y_send.at[int(up)],
                y_recv.at[k, int(up), c], device_id=target, device_id_type=MESH,
            ).start()

        @pl.when(core == 0)
        def _():
            planes(True, near)

        @pl.when(core == 1)
        def _():
            planes(False, near)

        @pl.when((core == 1) & (x < 3))
        def _():
            planes(True, far)

        @pl.when((core == 0) & (x > 0))
        def _():
            planes(False, far)

    def wait_for(ref, sem):
        pltpu.make_async_copy(ref, ref, sem).wait()

    def wait_halo(k, c):
        for side in range(2):
            wait_for(xrecv.at[k, side, c], x_recv.at[k, side, c])

        @pl.when(jnp.logical_not(bottom))
        def _():
            wait_for(fld.at[k, 0, c], y_recv.at[k, 1, c])

        @pl.when(jnp.logical_not(top))
        def _():
            wait_for(fld.at[k, 3, c], y_recv.at[k, 0, c])

    row = lax.broadcasted_iota(jnp.int32, (32, 256), 0) % 8

    def spread(v):
        return jnp.broadcast_to(v[:, None, :], (4, 8, 256)).reshape(32, 256)

    def spatial(k, c, p, q):
        part = pl.ds(q * 32, 32)
        v = fld[k, 1 + p, c, part]
        edge = pl.ds(pl.multiple_of(16 * p, 16), 16)
        before = spread(xrecv[k, 0, c, edge][q * 4 : q * 4 + 4])
        after = spread(xrecv[k, 1, c, edge][q * 4 : q * 4 + 4])
        xm = jnp.where(row == 0, before, pltpu.roll(v, 1, 0))
        xp = jnp.where(row == 7, after, pltpu.roll(v, 31, 0))
        total = fld[k, 2 + p, c, part] + fld[k, p, c, part] + xm + xp
        total = total + pltpu.roll(v, 1, 1) + pltpu.roll(v, 255, 1) - 6.0 * v
        plane = (4 * x + 2 * core + p).astype(F32)
        speed = 2.0 * (plane + 0.5) / 16 - 1.0
        return part, total, speed * (0.5 * (xp - xm))

    def derive(k, c):
        for p in range(2):
            dbuf[p] = jnp.dot(
                kmat[...], fld[k, 1 + p, c], preferred_element_type=F32,
                precision=lax.Precision.HIGHEST,
            )

    def symmetrize(c):
        wait_for(rbuf[c], in_recv.at[c])

        def take(p, t, half):
            return rbuf[c][p, inv[t % 16], half]

        for p in range(2):
            other = jnp.concatenate([take(p, t + 8, 1) for t in range(16)], axis=0)
            own = jnp.concatenate([take(p, t, 0) for t in range(16)], axis=0)
            fld[0, 1 + p, c] = 0.5 * (own + signed(c, reflect_z(other)))
        send_halo(0, c)

    def residual(k, c, omega):
        wait_halo(k, c)
        derive(k, c)

        def body(p, carry):
            for q in range(4):
                part, lap, advect = spatial(k, c, p, q)
                d = dbuf[p, part]
                value = omega * d - VISCOSITY * lap + advect
                fld[k + 1, 1 + p, c, part] = value
                acc[k // 2] += value * d
            return carry

        lax.fori_loop(0, 2, body, 0)
        send_halo(k + 1, c)

    def descend(k, c, omega, store):
        wait_halo(k, c)
        derive(k, c)

        def body(p, carry):
            for q in range(4):
                part, lap, advect = spatial(k, c, p, q)
                rate = omega * dbuf[p, part] + VISCOSITY * lap + advect
                store(p, part, fld[k - 1, 1 + p, c, part] + DESCENT * rate)
            return carry

        lax.fori_loop(0, 2, body, 0)

    def next_field(c, omega):
        def store(p, part, value):
            fld[2, 1 + p, c, part] = value

        descend(1, c, omega, store)
        send_halo(2, c)

    stages = (
        (0, 8, z * 2 + core, lambda r: device(x, y, r // 2, r % 2)),
        (8, 4, y, lambda r: device(x, r, z, core)),
        (12, 4, x, lambda r: device(r, y, z, core)),
    )

    def drift_send(it, stage, tile):
        base, size, rank, of = stages[stage]
        drift[it, base + rank] = tile
        for k in range(1, size):
            pltpu.make_async_remote_copy(
                drift.at[it, base + rank], drift.at[it, base + rank], d_send,
                d_recv.at[it, stage], device_id=of((rank + k) % size), device_id_type=MESH,
            ).start()

    def drift_sum(it, stage):
        base, size, _, _ = stages[stage]
        wait_for(drift.at[it, pl.ds(base, size - 1)], d_recv.at[it, stage])
        tile = drift[it, base]
        for k in range(1, size):
            tile = tile + drift[it, base + k]
        return tile

    def drift_start(it):
        a = acc[it]
        tile = a[0:8] + a[8:16] + a[16:24] + a[24:32]
        drift_send(it, 0, tile[:, :128] + tile[:, 128:])

    entries = 16 * 3 * 16 * 256 * 256

    def drift_end(it, omega):
        return omega - FREQUENCY_RATE * (jnp.sum(drift_sum(it, 2)) / (entries // 2))

    def send_out(o, c, source):
        for p in range(2):
            value = source(p)[...]
            turned = signed(c, reflect_z(value)).reshape(16, 8, 256)
            mbuf[p, 0] = value.reshape(16, 8, 256)
            mbuf[p, 1, 0:8] = turned[8:16]
            mbuf[p, 1, 8:16] = turned[0:8]

            def build(s, carry):
                t = times[s]
                at = p * 8 + s // 2
                obuf[o, c, at, s % 2, 0] = mbuf[p, 0, t]
                obuf[o, c, at, s % 2, 1] = mbuf[p, 1, t]
                return carry

            lax.fori_loop(0, 16, build, 0)

        def body(k, carry):
            p = k % 2
            di = (inst + k // 2) % 8
            ds = x * 4 + core * 2 + p
            src = obuf.at[o, c, p * 8 + di]
            dst = outs[o].at[:, c, :, myj]
            mine = (di == inst) & (ds == space)

            @pl.when(mine)
            def _():
                pltpu.make_async_copy(src, dst, o_recv.at[o]).start()

            @pl.when(jnp.logical_not(mine))
            def _():
                pltpu.make_async_remote_copy(
                    src, dst, o_send.at[o], o_recv.at[o], device_id=(di, ds), device_id_type=MESH
                ).start()

            return carry

        lax.fori_loop(0, 16, body, 0)

    acc[...] = jnp.zeros(acc.shape, F32)
    omega = freq[0]
    symmetrize(0)
    residual(0, 0, omega)
    symmetrize(1)
    next_field(0, omega)
    residual(0, 1, omega)
    symmetrize(2)
    next_field(1, omega)
    residual(0, 2, omega)
    drift_start(0)
    next_field(2, omega)
    drift_send(0, 1, drift_sum(0, 0))
    drift_send(0, 2, drift_sum(0, 1))
    omega = drift_end(0, omega)
    for c in range(3):
        residual(2, c, omega)
        send_out(0, c, lambda p: fld.at[3, 1 + p, c])
    drift_start(1)
    for c in range(3):

        def keep(p, part, value):
            orb[p, part] = value

        descend(3, c, omega, keep)
        send_out(1, c, lambda p: orb.at[p])
    drift_send(1, 1, drift_sum(1, 0))
    drift_send(1, 2, drift_sum(1, 1))
    fout[0] = drift_end(1, omega)

    for o in range(2):
        wait_for(outs[o], o_recv.at[o])
    part = pl.ds(0, 15)

    @pl.when(core == yhi)
    def _():
        wait_for(vel.at[:, :, :, part], in_send)
        for o in range(2):
            wait_for(obuf.at[o, :, part], o_send.at[o])

    @pl.when(core != yhi)
    def _():
        wait_for(vel, in_send)
        for o in range(2):
            wait_for(obuf.at[o], o_send.at[o])

    wait_for(xsend, x_send)

    @pl.when(jnp.logical_not(top))
    def _():
        wait_for(fld.at[:, 2], y_send.at[1])

    @pl.when(jnp.logical_not(bottom))
    def _():
        wait_for(fld.at[:, 1], y_send.at[0])

    wait_for(drift.at[:, pl.ds(0, 13)], d_send)


def shards(velocity, frequency, slot_time, mirror_rows):
    cut = (2, 3, 2, 16, 8, 256)
    whole = jax.ShapeDtypeStruct(cut, F32)
    smem = pl.BlockSpec(memory_space=pltpu.SMEM)
    vmem = pl.BlockSpec(memory_space=pltpu.VMEM)
    hbm = pl.BlockSpec(memory_space=pl.ANY)
    dma = pltpu.SemaphoreType.DMA
    orbit, defect, new = pl.pallas_call(
        kernel,
        out_shape=(whole, whole, jax.ShapeDtypeStruct((1,), F32)),
        in_specs=[smem, smem, vmem, hbm],
        out_specs=(hbm, hbm, smem),
        scratch_shapes=[
            pltpu.VMEM((2, 16, 2, 8, 256), F32),
            pltpu.VMEM((2, 16, 2, 8, 256), F32),
            pltpu.VMEM((2, 16, 2, 8, 256), F32),
            pltpu.VMEM((4, 4, 3, 128, 256), F32),
            pltpu.VMEM((2, 128, 256), F32),
            pltpu.VMEM((4, 2, 3, 32, 256), F32),
            pltpu.VMEM((4, 2, 3, 32, 256), F32),
            pltpu.VMEM((2, 3, 16, 2, 2, 8, 256), F32),
            pltpu.VMEM((2, 2, 16, 8, 256), F32),
            pltpu.VMEM((2, 128, 256), F32),
            pltpu.VMEM((256, 256), jnp.bfloat16),
            pltpu.VMEM((128, 128), F32),
            pltpu.VMEM((2, 32, 256), F32),
            pltpu.VMEM((2, 16, 8, 128), F32),
            pltpu.SMEM((16,), jnp.int32),
            dma,
            dma((3,)),
            dma,
            dma((4, 2, 3)),
            dma((2,)),
            dma((4, 2, 3)),
            dma((2,)),
            dma((2,)),
            dma,
            dma((2, 3)),
        ],
        compiler_params=pltpu.CompilerParams(
            collective_id=0, has_side_effects=True, vmem_limit_bytes=40 * 1024 * 1024
        ),
    )(frequency, slot_time, mirror_rows.reshape(1, 256), velocity.reshape(cut))
    return orbit.reshape(velocity.shape), defect.reshape(velocity.shape), new


def solution(mesh):
    spread = P("inst", None, "space", None, None)
    return jax.shard_map(
        shards, mesh=mesh, in_specs=(spread, P(), P(), P()), out_specs=(spread, spread, P()),
        check_vma=False,
    )
```

time: 874 us -> 107 us (0.12)
  waiting for transfers between devices: 377 us -> 0 us
  blocking collectives: 205 us -> 0 us
  local copies, waits for them, and re-layouts: 177 us -> 5.02 us
  Pallas kernels: 0 us -> 96.7 us
  other arithmetic: 31.6 us -> 0 us
  starting transfers between devices: 29.1 us -> 0 us
  matrix products: 27.2 us -> 0 us
  between operations: 18.2 us -> 3.03 us
    all_gather x2 -> x0, waiting for transfers between devices: 280 us -> none  [shards(): lax.all_gather(field, 'inst', axis=0, tiled=True)]
    psum x2 -> x0, blocking collectives: 205 us -> none  [shards(): drift = lax.psum(jnp.sum(defect * derivative), ('inst', 'space'))]
    ppermute x8 -> x0, waiting for transfers between devices: 96.9 us -> none  [the longest x4 51.7 us: extended(): before = lax.ppermute(last, axis, up)]
    pallas_call x0 -> x1, Pallas kernels: none -> 96.7 us  [shards(): pl.pallas_call(kernel, out_shape=(whole, whole, jax.ShapeDtypeStruct((1,)...]
    rev x6 -> x0, local copies, waits for them, and re-layouts: 47.2 us -> none  [reflect_halves(): flipped = jnp.take(jnp.flip(halves, axis=-3), mirror, axis=-1)]
    unnamed x70 -> x8, local copies, waits for them, and re-layouts: 51.8 us -> 5.02 us
    gather x12 -> x0, local copies, waits for them, and re-layouts: 39.1 us -> none  [reflect_halves(): flipped = jnp.take(jnp.flip(halves, axis=-3), mirror, axis=-1)]
    ppermute x8 -> x0, starting transfers between devices: 29 us -> none  [the longest x4 19.3 us: extended(): before = lax.ppermute(last, axis, up)]
  transfers between devices with their start and end apart: 10 -> 0, of which waited for: 6 -> 0; matrix products, arithmetic and copies ran while one was open for 2% -> 0% of each run, Pallas kernels for 0% -> 0%
where the time goes in v1:
time: 107 us; the launch traced here: 105 us
  Pallas kernels  96.7 us (90%)
  local copies, waits for them, and re-layouts  5.02 us (5%)
  between operations  3.03 us (3%)
    pallas_call x1, Pallas kernels, shards(): pl.pallas_call(kernel, out_shape=(whole, whole, jax.ShapeDtypeStruct((1,)...  96.7 us
    unnamed x8, local copies, waits for them, and re-layouts  5.02 us

profile of v1, /device:TPU:1, one launch (start us, length us, event | category | flops | bytes accessed | tf_op | source)
XLA Modules:
  0.0 104.8 jit_solution(4579836779959545832)
XLA Ops:
  1.3 0.0 copy-start
  1.3 1.4 %copy-done = f32[2,3,1,256,256]{4,3,2,1,0:T(8,128)S(1)} copy-done((f32[2,3,1,256,256]{4,3,2,1,0:T(8,128)S(1)}, f32[2,3,1,256,256]{4,3,2,1,0:T(8,128)}, u32[]{:S(2)}) %copy-start) | copy-done | bytes 1572888
  2.7 0.0 copy-start.1
  2.7 0.7 copy-done.1
  3.4 0.0 copy-start.2
  3.4 0.7 copy-done.2
  4.0 96.7 %shard_map.67 = (f32[2,3,2,16,8,256]{5,4,3,2,1,0:T(8,128)S(1)}, f32[2,3,2,16,8,256]{5,4,3,2,1,0:T(8,128)S(1)}, f32[1]{0:T(128)}) custom-call(f32[1]{0:T(128)S(6)} %copy.12.freq, s32[16]{0:T(128)S(1)} %copy-done.2, s32[1,256]{1,0:T(1,128)S(1)} %bitcast.11, f32[2,3,2,16,8,256]{5,4,3,2,1,0:T(8,128)S(1)} %bitcast.8), custom_call_target="tpu_custom_call" | custom-call | tf_op jit(solution)/shard_map/pallas_call | solution.py:416
  100.7 1.1 %copy.13 = f32[2,3,1,256,256]{4,3,2,1,0:T(8,128)} copy(f32[2,3,1,256,256]{4,3,2,1,0:T(8,128)S(1)} %bitcast.10) | data formatting | bytes 3145728
  101.9 1.1 %copy.14 = f32[2,3,1,256,256]{4,3,2,1,0:T(8,128)} copy(f32[2,3,1,256,256]{4,3,2,1,0:T(8,128)S(1)} %bitcast.9) | data formatting | bytes 3145728
Async XLA Ops:
  1.3 1.4 %copy-start = (f32[2,3,1,256,256]{4,3,2,1,0:T(8,128)S(1)}, f32[2,3,1,256,256]{4,3,2,1,0:T(8,128)}, u32[]{:S(2)}) copy-start(f32[2,3,1,256,256]{4,3,2,1,0:T(8,128)} %param.4) | copy-start | bytes 4718596
  2.7 0.7 copy-start.1
  3.4 0.7 copy-start.2

commit v2 on v1

--- a/solution.py
+++ b/solution.py
@@ -34,9 +34,9 @@
 
 
 def kernel(
-    freq, times, mirror, vel, orbit, defect, fout,
+    freq_in, times_in, mirror_in, vel, orbit, defect, fout, freq, times, mirror,
     rbuf0, rbuf1, rbuf2, fld, orb, xsend, xrecv, obuf, mbuf, dbuf, mat, kmat, acc, drift, inv,
-    in_send, in_recv, x_send, x_recv, y_send, y_recv, o_send, o_recv, d_send, d_recv,
+    small, in_send, in_recv, x_send, x_recv, y_send, y_recv, o_send, o_recv, d_send, d_recv,
 ):
     inst = lax.axis_index("inst")
     space = lax.axis_index("space")
@@ -69,6 +69,44 @@
     near = device(x, y, z, 1 - core)
     pl.semaphore_signal(barrier, inc=1, device_id=far, device_id_type=MESH)
 
+    fetches = [
+        pltpu.make_async_copy(src, dst, small.at[k])
+        for k, (src, dst) in enumerate(
+            ((freq_in, freq), (times_in, times), (mirror_in, mirror))
+        )
+    ]
+    for copy in fetches:
+        copy.start()
+    pl.semaphore_wait(barrier, 35)
+
+    def send_in(c):
+        def body(k, carry):
+            j = (k + myj) % 16
+            cy, cz = chip_of(j)
+            di, ds = device(x, cy, cz, yhi)
+            src = vel.at[:, c, :, j]
+            dst = rbuf[c].at[core, pl.ds(2 * inst, 2)]
+            mine = (di == inst) & (ds == space)
+
+            @pl.when(mine)
+            def _():
+                pltpu.make_async_copy(src, dst, in_recv.at[c]).start()
+
+            @pl.when(jnp.logical_not(mine))
+            def _():
+                pltpu.make_async_remote_copy(
+                    src, dst, in_send, in_recv.at[c], device_id=(di, ds), device_id_type=MESH
+                ).start()
+
+            return carry
+
+        lax.fori_loop(0, 16, body, 0)
+
+    for c in range(3):
+        send_in(c)
+
+    for copy in fetches:
+        copy.wait()
     mat[...] = (
         lax.broadcasted_iota(jnp.int32, (256, 256), 0) == mirror[...]
     ).astype(F32).astype(jnp.bfloat16)
@@ -98,34 +136,6 @@
     @pl.when(top)
     def _():
         fld[:, 3] = jnp.zeros((4, 3, 128, 256), F32)
-
-    pl.semaphore_wait(barrier, 35)
-
-    def send_in(c):
-        def body(k, carry):
-            j = (k + myj) % 16
-            cy, cz = chip_of(j)
-            di, ds = device(x, cy, cz, yhi)
-            src = vel.at[:, c, :, j]
-            dst = rbuf[c].at[core, pl.ds(2 * inst, 2)]
-            mine = (di == inst) & (ds == space)
-
-            @pl.when(mine)
-            def _():
-                pltpu.make_async_copy(src, dst, in_recv.at[c]).start()
-
-            @pl.when(jnp.logical_not(mine))
-            def _():
-                pltpu.make_async_remote_copy(
-                    src, dst, in_send, in_recv.at[c], device_id=(di, ds), device_id_type=MESH
-                ).start()
-
-            return carry
-
-        lax.fori_loop(0, 16, body, 0)
-
-    for c in range(3):
-        send_in(c)
 
     def reflect_z(v):
         high = v.astype(jnp.bfloat16)
@@ -349,18 +359,16 @@
 
     acc[...] = jnp.zeros(acc.shape, F32)
     omega = freq[0]
-    symmetrize(0)
-    residual(0, 0, omega)
-    symmetrize(1)
+    for c in range(3):
+        symmetrize(c)
+    for c in range(3):
+        residual(0, c, omega)
+    drift_start(0)
     next_field(0, omega)
-    residual(0, 1, omega)
-    symmetrize(2)
+    drift_send(0, 1, drift_sum(0, 0))
     next_field(1, omega)
-    residual(0, 2, omega)
-    drift_start(0)
+    drift_send(0, 2, drift_sum(0, 1))
     next_field(2, omega)
-    drift_send(0, 1, drift_sum(0, 0))
-    drift_send(0, 2, drift_sum(0, 1))
     omega = drift_end(0, omega)
     for c in range(3):
         residual(2, c, omega)
@@ -375,7 +383,10 @@
         send_out(1, c, lambda p: orb.at[p])
     drift_send(1, 1, drift_sum(1, 0))
     drift_send(1, 2, drift_sum(1, 1))
-    fout[0] = drift_end(1, omega)
+    freq[0] = drift_end(1, omega)
+    result = pltpu.make_async_copy(freq, fout, small.at[0])
+    result.start()
+    result.wait()
 
     for o in range(2):
         wait_for(outs[o], o_recv.at[o])
@@ -406,19 +417,39 @@
     wait_for(drift.at[:, pl.ds(0, 13)], d_send)
 
 
+def finish(orbit, defect, new, orbit_out, defect_out, new_out, one, sems):
+    first = pltpu.make_async_copy(new, one, sems.at[0])
+    first.start()
+    copies = [
+        pltpu.make_async_copy(src.at[s], dst.at[s], sems.at[1 + 2 * k + s])
+        for k, (src, dst) in enumerate(((orbit, orbit_out), (defect, defect_out)))
+        for s in range(2)
+    ]
+    for copy in copies:
+        copy.start()
+    first.wait()
+    copies.append(pltpu.make_async_copy(one, new_out, sems.at[5]))
+    copies[-1].start()
+    for copy in copies:
+        copy.wait()
+
+
 def shards(velocity, frequency, slot_time, mirror_rows):
     cut = (2, 3, 2, 16, 8, 256)
     whole = jax.ShapeDtypeStruct(cut, F32)
-    smem = pl.BlockSpec(memory_space=pltpu.SMEM)
+    shapes = (whole, whole, jax.ShapeDtypeStruct((1,), F32))
+    hbm = pl.BlockSpec(memory_space=pltpu.HBM)
     vmem = pl.BlockSpec(memory_space=pltpu.VMEM)
-    hbm = pl.BlockSpec(memory_space=pl.ANY)
     dma = pltpu.SemaphoreType.DMA
-    orbit, defect, new = pl.pallas_call(
+    results = pl.pallas_call(
         kernel,
-        out_shape=(whole, whole, jax.ShapeDtypeStruct((1,), F32)),
-        in_specs=[smem, smem, vmem, hbm],
-        out_specs=(hbm, hbm, smem),
+        out_shape=(pltpu.VMEM(cut, F32), pltpu.VMEM(cut, F32), shapes[2]),
+        in_specs=[hbm] * 4,
+        out_specs=(vmem, vmem, hbm),
         scratch_shapes=[
+            pltpu.SMEM((1,), F32),
+            pltpu.SMEM((16,), jnp.int32),
+            pltpu.VMEM((1, 256), jnp.int32),
             pltpu.VMEM((2, 16, 2, 8, 256), F32),
             pltpu.VMEM((2, 16, 2, 8, 256), F32),
             pltpu.VMEM((2, 16, 2, 8, 256), F32),
@@ -434,6 +465,7 @@
             pltpu.VMEM((2, 32, 256), F32),
             pltpu.VMEM((2, 16, 8, 128), F32),
             pltpu.SMEM((16,), jnp.int32),
+            dma((3,)),
             dma,
             dma((3,)),
             dma,
@@ -448,7 +480,18 @@
         compiler_params=pltpu.CompilerParams(
             collective_id=0, has_side_effects=True, vmem_limit_bytes=40 * 1024 * 1024
         ),
-    )(frequency, slot_time, mirror_rows.reshape(1, 256), velocity.reshape(cut))
+    )(frequency, *[
+        pltpu.with_memory_space_constraint(v, pltpu.HBM)
+        for v in (slot_time, mirror_rows.reshape(1, 256), velocity.reshape(cut))
+    ])
+    orbit, defect, new = pl.pallas_call(
+        finish,
+        out_shape=shapes,
+        in_specs=[vmem, vmem, hbm],
+        out_specs=(hbm,) * 3,
+        scratch_shapes=[pltpu.SMEM((1,), F32), dma((6,))],
+        compiler_params=pltpu.CompilerParams(vmem_limit_bytes=4 * 1024 * 1024),
+    )(*results)
     return orbit.reshape(velocity.shape), defect.reshape(velocity.shape), new
 
 

time: 107 us -> 93.6 us (0.87)
  the two profiles are of different devices: /device:TPU:1 before, /device:TPU:0 now
where the time goes in v2:
time: 93.6 us; the launch traced here: 93.4 us
  Pallas kernels  92.2 us (99%)
  between operations  1.28 us (1%)
    pallas_call x1, Pallas kernels, shards(): pl.pallas_call(kernel, out_shape=(pltpu.VMEM(cut, F32), pltpu.VMEM(cut, F...  89.8 us
    pallas_call x1, Pallas kernels, shards(): pl.pallas_call(finish, out_shape=shapes, in_specs=[vmem, vmem, hbm], out_...  2.35 us

profile of v2, /device:TPU:0, one launch (start us, length us, event | category | flops | bytes accessed | tf_op | source)
XLA Modules:
  0.0 93.4 jit_solution(3870297139448279030)
XLA Ops:
  1.3 89.8 %shard_map.67 = (f32[2,3,2,16,8,256]{5,4,3,2,1,0:T(8,128)S(1)}, f32[2,3,2,16,8,256]{5,4,3,2,1,0:T(8,128)S(1)}, f32[1]{0:T(128)}) custom-call(f32[1]{0:T(128)S(6)} %copy.9.freq_in, s32[16]{0:T(128)} %times_in.1, s32[1,256]{1,0:T(1,128)} %bitcast.9, f32[2,3,2,16,8,256]{5,4,3,2,1,0:T(8,128)} %bitcast.8), custom_call_target="tpu_custom_call" | custom-call | tf_op jit(solution)/shard_map/pallas_call | solution.py:444
  91.1 2.4 %shard_map.68 = (f32[2,3,2,16,8,256]{5,4,3,2,1,0:T(8,128)}, f32[2,3,2,16,8,256]{5,4,3,2,1,0:T(8,128)}, f32[1]{0:T(128)}) custom-call(f32[2,3,2,16,8,256]{5,4,3,2,1,0:T(8,128)S(1)} %get-tuple-element.9.orbit, f32[2,3,2,16,8,256]{5,4,3,2,1,0:T(8,128)S(1)} %get-tuple-element.10.defect, f32[1]{0:T(128)} %get-tuple-element.11.new), custom_call_target="tpu_custom_call" | custom-call | tf_op jit(solution)/shard_map/pallas_call | solution.py:487

commit v3 on v2

--- a/solution.py
+++ b/solution.py
@@ -61,10 +61,15 @@
         return carry
 
     lax.fori_loop(1, 32, greet_chip, 0)
-    for k in range(1, 4):
+
+    def greet_plane(k, carry):
+        dx = (x + 1 + k // 4) % 4
         pl.semaphore_signal(
-            barrier, inc=1, device_id=device((x + k) % 4, y, z, core), device_id_type=MESH
+            barrier, inc=1, device_id=device(dx, (y + k) % 4, z, core), device_id_type=MESH
         )
+        return carry
+
+    lax.fori_loop(0, 12, greet_plane, 0)
     far = device((x + jnp.where(core == 1, 1, 3)) % 4, y, z, 1 - core)
     near = device(x, y, z, 1 - core)
     pl.semaphore_signal(barrier, inc=1, device_id=far, device_id_type=MESH)
@@ -77,7 +82,7 @@
     ]
     for copy in fetches:
         copy.start()
-    pl.semaphore_wait(barrier, 35)
+    pl.semaphore_wait(barrier, 44)
 
     def send_in(c):
         def body(k, carry):
@@ -232,7 +237,7 @@
 
     def derive(k, c):
         for p in range(2):
-            dbuf[p] = jnp.dot(
+            dbuf[c, p] = jnp.dot(
                 kmat[...], fld[k, 1 + p, c], preferred_element_type=F32,
                 precision=lax.Precision.HIGHEST,
             )
@@ -249,30 +254,54 @@
             fld[0, 1 + p, c] = 0.5 * (own + signed(c, reflect_z(other)))
         send_halo(0, c)
 
-    def residual(k, c, omega):
+    def residual(c, omega):
+        wait_halo(0, c)
+        derive(0, c)
+
+        def body(p, carry):
+            for q in range(4):
+                part, lap, advect = spatial(0, c, p, q)
+                d = dbuf[c, p, part]
+                value = omega * d - VISCOSITY * lap + advect
+                fld[1, 1 + p, c, part] = value
+                acc[0] += value * d
+            return carry
+
+        lax.fori_loop(0, 2, body, 0)
+
+    def prepare(c):
+        wait_halo(2, c)
+        derive(2, c)
+
+        def body(p, carry):
+            for q in range(4):
+                part, lap, advect = spatial(2, c, p, q)
+                fld[3, 1 + p, c, part] = advect - VISCOSITY * lap
+            return carry
+
+        lax.fori_loop(0, 2, body, 0)
+
+    def complete(c, omega):
+        def body(p, carry):
+            for q in range(4):
+                part = pl.ds(q * 32, 32)
+                d = dbuf[c, p, part]
+                value = omega * d + fld[3, 1 + p, c, part]
+                fld[3, 1 + p, c, part] = value
+                acc[1] += value * d
+            return carry
+
+        lax.fori_loop(0, 2, body, 0)
+        send_halo(3, c)
+
+    def descend(k, c, omega, store):
         wait_halo(k, c)
         derive(k, c)
 
         def body(p, carry):
             for q in range(4):
                 part, lap, advect = spatial(k, c, p, q)
-                d = dbuf[p, part]
-                value = omega * d - VISCOSITY * lap + advect
-                fld[k + 1, 1 + p, c, part] = value
-                acc[k // 2] += value * d
-            return carry
-
-        lax.fori_loop(0, 2, body, 0)
-        send_halo(k + 1, c)
-
-    def descend(k, c, omega, store):
-        wait_halo(k, c)
-        derive(k, c)
-
-        def body(p, carry):
-            for q in range(4):
-                part, lap, advect = spatial(k, c, p, q)
-                rate = omega * dbuf[p, part] + VISCOSITY * lap + advect
+                rate = omega * dbuf[c, p, part] + VISCOSITY * lap + advect
                 store(p, part, fld[k - 1, 1 + p, c, part] + DESCENT * rate)
             return carry
 
@@ -287,18 +316,21 @@
 
     stages = (
         (0, 8, z * 2 + core, lambda r: device(x, y, r // 2, r % 2)),
-        (8, 4, y, lambda r: device(x, r, z, core)),
-        (12, 4, x, lambda r: device(r, y, z, core)),
+        (8, 16, x * 4 + y, lambda r: device(r // 4, r % 4, z, core)),
     )
 
     def drift_send(it, stage, tile):
         base, size, rank, of = stages[stage]
         drift[it, base + rank] = tile
-        for k in range(1, size):
+
+        def body(k, carry):
             pltpu.make_async_remote_copy(
                 drift.at[it, base + rank], drift.at[it, base + rank], d_send,
                 d_recv.at[it, stage], device_id=of((rank + k) % size), device_id_type=MESH,
             ).start()
+            return carry
+
+        lax.fori_loop(1, size, body, 0)
 
     def drift_sum(it, stage):
         base, size, _, _ = stages[stage]
@@ -316,7 +348,7 @@
     entries = 16 * 3 * 16 * 256 * 256
 
     def drift_end(it, omega):
-        return omega - FREQUENCY_RATE * (jnp.sum(drift_sum(it, 2)) / (entries // 2))
+        return omega - FREQUENCY_RATE * (jnp.sum(drift_sum(it, 1)) / (entries // 2))
 
     def send_out(o, c, source):
         for p in range(2):
@@ -326,63 +358,68 @@
             mbuf[p, 1, 0:8] = turned[8:16]
             mbuf[p, 1, 8:16] = turned[0:8]
 
-            def build(s, carry):
-                t = times[s]
-                at = p * 8 + s // 2
-                obuf[o, c, at, s % 2, 0] = mbuf[p, 0, t]
-                obuf[o, c, at, s % 2, 1] = mbuf[p, 1, t]
+            def build(i, carry):
+                for s in range(2):
+                    t = times[2 * i + s]
+                    obuf[o, c, p * 8 + i, s, 0] = mbuf[p, 0, t]
+                    obuf[o, c, p * 8 + i, s, 1] = mbuf[p, 1, t]
                 return carry
 
-            lax.fori_loop(0, 16, build, 0)
-
-        def body(k, carry):
-            p = k % 2
-            di = (inst + k // 2) % 8
-            ds = x * 4 + core * 2 + p
-            src = obuf.at[o, c, p * 8 + di]
-            dst = outs[o].at[:, c, :, myj]
-            mine = (di == inst) & (ds == space)
-
-            @pl.when(mine)
-            def _():
-                pltpu.make_async_copy(src, dst, o_recv.at[o]).start()
-
-            @pl.when(jnp.logical_not(mine))
-            def _():
-                pltpu.make_async_remote_copy(
-                    src, dst, o_send.at[o], o_recv.at[o], device_id=(di, ds), device_id_type=MESH
-                ).start()
-
-            return carry
-
-        lax.fori_loop(0, 16, body, 0)
+            lax.fori_loop(0, 8, build, 0)
+
+            def body(k, carry):
+                di = (inst + k) % 8
+                ds = x * 4 + core * 2 + p
+                src = obuf.at[o, c, p * 8 + di]
+                dst = outs[o].at[:, c, :, myj]
+                mine = (di == inst) & (ds == space)
+
+                @pl.when(mine)
+                def _():
+                    pltpu.make_async_copy(src, dst, o_recv.at[o]).start()
+
+                @pl.when(jnp.logical_not(mine))
+                def _():
+                    pltpu.make_async_remote_copy(
+                        src, dst, o_send.at[o], o_recv.at[o], device_id=(di, ds),
+                        device_id_type=MESH,
+                    ).start()
+
+                return carry
+
+            lax.fori_loop(0, 8, body, 0)
 
     acc[...] = jnp.zeros(acc.shape, F32)
     omega = freq[0]
     for c in range(3):
         symmetrize(c)
     for c in range(3):
-        residual(0, c, omega)
-    drift_start(0)
+        residual(c, omega)
+        if c == 2:
+            drift_start(0)
+        send_halo(1, c)
     next_field(0, omega)
     drift_send(0, 1, drift_sum(0, 0))
     next_field(1, omega)
-    drift_send(0, 2, drift_sum(0, 1))
     next_field(2, omega)
+    prepare(0)
     omega = drift_end(0, omega)
     for c in range(3):
-        residual(2, c, omega)
+        if c > 0:
+            prepare(c)
+        complete(c, omega)
+        if c == 2:
+            drift_start(1)
         send_out(0, c, lambda p: fld.at[3, 1 + p, c])
-    drift_start(1)
     for c in range(3):
 
         def keep(p, part, value):
             orb[p, part] = value
 
         descend(3, c, omega, keep)
+        if c == 0:
+            drift_send(1, 1, drift_sum(1, 0))
         send_out(1, c, lambda p: orb.at[p])
-    drift_send(1, 1, drift_sum(1, 0))
-    drift_send(1, 2, drift_sum(1, 1))
     freq[0] = drift_end(1, omega)
     result = pltpu.make_async_copy(freq, fout, small.at[0])
     result.start()
@@ -414,7 +451,7 @@
     def _():
         wait_for(fld.at[:, 1], y_send.at[0])
 
-    wait_for(drift.at[:, pl.ds(0, 13)], d_send)
+    wait_for(drift.at[:, pl.ds(0, 22)], d_send)
 
 
 def finish(orbit, defect, new, orbit_out, defect_out, new_out, one, sems):
@@ -459,11 +496,11 @@
             pltpu.VMEM((4, 2, 3, 32, 256), F32),
             pltpu.VMEM((2, 3, 16, 2, 2, 8, 256), F32),
             pltpu.VMEM((2, 2, 16, 8, 256), F32),
-            pltpu.VMEM((2, 128, 256), F32),
+            pltpu.VMEM((3, 2, 128, 256), F32),
             pltpu.VMEM((256, 256), jnp.bfloat16),
             pltpu.VMEM((128, 128), F32),
             pltpu.VMEM((2, 32, 256), F32),
-            pltpu.VMEM((2, 16, 8, 128), F32),
+            pltpu.VMEM((2, 24, 8, 128), F32),
             pltpu.SMEM((16,), jnp.int32),
             dma((3,)),
             dma,
@@ -475,7 +512,7 @@
             dma((2,)),
             dma((2,)),
             dma,
-            dma((2, 3)),
+            dma((2, 2)),
         ],
         compiler_params=pltpu.CompilerParams(
             collective_id=0, has_side_effects=True, vmem_limit_bytes=40 * 1024 * 1024

time: 93.6 us -> 88.6 us (0.947)
  the two profiles are of different devices: /device:TPU:0 before, /device:TPU:1 now
where the time goes in v3:
time: 88.6 us; the launch traced here: 88.5 us
  Pallas kernels  87.2 us (98%)
  between operations  1.28 us (1%)
    pallas_call x1, Pallas kernels, shards(): pl.pallas_call(kernel, out_shape=(pltpu.VMEM(cut, F32), pltpu.VMEM(cut, F...  84.9 us
    pallas_call x1, Pallas kernels, shards(): pl.pallas_call(finish, out_shape=shapes, in_specs=[vmem, vmem, hbm], out_...  2.35 us

profile of v3, /device:TPU:1, one launch (start us, length us, event | category | flops | bytes accessed | tf_op | source)
XLA Modules:
  0.0 88.5 jit_solution(5428561992967251481)
XLA Ops:
  1.3 84.9 %shard_map.67 = (f32[2,3,2,16,8,256]{5,4,3,2,1,0:T(8,128)S(1)}, f32[2,3,2,16,8,256]{5,4,3,2,1,0:T(8,128)S(1)}, f32[1]{0:T(128)}) custom-call(f32[1]{0:T(128)S(6)} %copy.9.freq_in, s32[16]{0:T(128)} %times_in.1, s32[1,256]{1,0:T(1,128)} %bitcast.9, f32[2,3,2,16,8,256]{5,4,3,2,1,0:T(8,128)} %bitcast.8), custom_call_target="tpu_custom_call" | custom-call | tf_op jit(solution)/shard_map/pallas_call | solution.py:481
  86.2 2.4 %shard_map.68 = (f32[2,3,2,16,8,256]{5,4,3,2,1,0:T(8,128)}, f32[2,3,2,16,8,256]{5,4,3,2,1,0:T(8,128)}, f32[1]{0:T(128)}) custom-call(f32[2,3,2,16,8,256]{5,4,3,2,1,0:T(8,128)S(1)} %get-tuple-element.9.orbit, f32[2,3,2,16,8,256]{5,4,3,2,1,0:T(8,128)S(1)} %get-tuple-element.10.defect, f32[1]{0:T(128)} %get-tuple-element.11.new), custom_call_target="tpu_custom_call" | custom-call | tf_op jit(solution)/shard_map/pallas_call | solution.py:524

commit v4 on v3

--- a/solution.py
+++ b/solution.py
@@ -50,30 +50,21 @@
     rbuf = (rbuf0, rbuf1, rbuf2)
 
     barrier = pltpu.get_barrier_semaphore()
-    place = myj * 2 + core
-
-    def greet_chip(k, carry):
-        d = (k + place) % 32
-        cy, cz = chip_of(d // 2)
-        pl.semaphore_signal(
-            barrier, inc=1, device_id=device(x, cy, cz, d % 2), device_id_type=MESH
-        )
-        return carry
-
-    lax.fori_loop(1, 32, greet_chip, 0)
-
-    def greet_plane(k, carry):
-        dx = (x + 1 + k // 4) % 4
-        pl.semaphore_signal(
-            barrier, inc=1, device_id=device(dx, (y + k) % 4, z, core), device_id_type=MESH
-        )
-        return carry
-
-    lax.fori_loop(0, 12, greet_plane, 0)
+
+    steps = sorted(
+        ((dy, dz, dc) for dy in range(4) for dz in range(4) for dc in range(2)),
+        key=lambda d: -min(d[0], 4 - d[0]) - min(d[1], 4 - d[1]),
+    )
+    friends = [
+        device(x, (y + dy) % 4, (z + dz) % 4, (core + dc) % 2)
+        for dy, dz, dc in steps if dy + dz > 0
+    ]
+    friends += [device((x + 1 + k // 2) % 4, y, z, (core + k) % 2) for k in (2, 3, 0, 1, 4, 5)]
+    friends += [device(x, y, z, 1 - core)]
+    for friend in friends:
+        pl.semaphore_signal(barrier, inc=1, device_id=friend, device_id_type=MESH)
     far = device((x + jnp.where(core == 1, 1, 3)) % 4, y, z, 1 - core)
     near = device(x, y, z, 1 - core)
-    pl.semaphore_signal(barrier, inc=1, device_id=far, device_id_type=MESH)
-
     fetches = [
         pltpu.make_async_copy(src, dst, small.at[k])
         for k, (src, dst) in enumerate(
@@ -82,7 +73,7 @@
     ]
     for copy in fetches:
         copy.start()
-    pl.semaphore_wait(barrier, 44)
+    pl.semaphore_wait(barrier, len(friends))
 
     def send_in(c):
         def body(k, carry):
@@ -158,6 +149,29 @@
     right = chip_of((myj + 1) % 16)
 
     def send_halo(k, c):
+        def planes(up, target):
+            src, dst = (2, 0) if up else (1, 3)
+            pltpu.make_async_remote_copy(
+                fld.at[k, src, c], fld.at[k, dst, c], y_send.at[int(up)],
+                y_recv.at[k, int(up), c], device_id=target, device_id_type=MESH,
+            ).start()
+
+        @pl.when(core == 0)
+        def _():
+            planes(True, near)
+
+        @pl.when(core == 1)
+        def _():
+            planes(False, near)
+
+        @pl.when((core == 1) & (x < 3))
+        def _():
+            planes(True, far)
+
+        @pl.when((core == 0) & (x > 0))
+        def _():
+            planes(False, far)
+
         for p in range(2):
             part = pl.ds(16 * p, 16)
             tiles = fld[k, 1 + p, c].reshape(16, 8, 256)
@@ -178,29 +192,6 @@
                 x_recv.at[k, 1 - side, c], device_id=device(x, cy, cz, core), device_id_type=MESH,
             ).start()
 
-        def planes(up, target):
-            src, dst = (2, 0) if up else (1, 3)
-            pltpu.make_async_remote_copy(
-                fld.at[k, src, c], fld.at[k, dst, c], y_send.at[int(up)],
-                y_recv.at[k, int(up), c], device_id=target, device_id_type=MESH,
-            ).start()
-
-        @pl.when(core == 0)
-        def _():
-            planes(True, near)
-
-        @pl.when(core == 1)
-        def _():
-            planes(False, near)
-
-        @pl.when((core == 1) & (x < 3))
-        def _():
-            planes(True, far)
-
-        @pl.when((core == 0) & (x > 0))
-        def _():
-            planes(False, far)
-
     def wait_for(ref, sem):
         pltpu.make_async_copy(ref, ref, sem).wait()
 
@@ -221,19 +212,35 @@
     def spread(v):
         return jnp.broadcast_to(v[:, None, :], (4, 8, 256)).reshape(32, 256)
 
-    def spatial(k, c, p, q):
+    def speed_of(p):
+        plane = (4 * x + 2 * core + p).astype(F32)
+        return 2.0 * (plane + 0.5) / 16 - 1.0
+
+    def inner(k, c, p, q, scale):
         part = pl.ds(q * 32, 32)
         v = fld[k, 1 + p, c, part]
+        xm = jnp.where(row == 0, 0.0, pltpu.roll(v, 1, 0))
+        xp = jnp.where(row == 7, 0.0, pltpu.roll(v, 31, 0))
+        total = fld[k, 2 - p, c, part] + xm + xp
+        total = total + pltpu.roll(v, 1, 1) + pltpu.roll(v, 255, 1) - 6.0 * v
+        return part, scale * total + speed_of(p) * (0.5 * (xp - xm))
+
+    def outer(k, c, p, q, scale):
+        part = pl.ds(q * 32, 32)
         edge = pl.ds(pl.multiple_of(16 * p, 16), 16)
-        before = spread(xrecv[k, 0, c, edge][q * 4 : q * 4 + 4])
-        after = spread(xrecv[k, 1, c, edge][q * 4 : q * 4 + 4])
-        xm = jnp.where(row == 0, before, pltpu.roll(v, 1, 0))
-        xp = jnp.where(row == 7, after, pltpu.roll(v, 31, 0))
-        total = fld[k, 2 + p, c, part] + fld[k, p, c, part] + xm + xp
-        total = total + pltpu.roll(v, 1, 1) + pltpu.roll(v, 255, 1) - 6.0 * v
-        plane = (4 * x + 2 * core + p).astype(F32)
-        speed = 2.0 * (plane + 0.5) / 16 - 1.0
-        return part, total, speed * (0.5 * (xp - xm))
+        half = 0.5 * speed_of(p)
+        before = spread((scale - half) * xrecv[k, 0, c, edge][q * 4 : q * 4 + 4])
+        after = spread((scale + half) * xrecv[k, 1, c, edge][q * 4 : q * 4 + 4])
+        rows = jnp.where(row == 0, before, jnp.where(row == 7, after, 0.0))
+        return part, scale * fld[k, 3 * p, c, part] + rows
+
+    def tiles(body):
+        def step(p, carry):
+            for q in range(4):
+                body(p, q)
+            return carry
+
+        lax.fori_loop(0, 2, step, 0)
 
     def derive(k, c):
         for p in range(2):
@@ -254,69 +261,84 @@
             fld[0, 1 + p, c] = 0.5 * (own + signed(c, reflect_z(other)))
         send_halo(0, c)
 
-    def residual(c, omega):
+    def residual_inner(c, omega):
+        derive(0, c)
+
+        def body(p, q):
+            part, value = inner(0, c, p, q, -VISCOSITY)
+            fld[1, 1 + p, c, part] = omega * dbuf[c, p, part] + value
+
+        tiles(body)
+
+    def residual_outer(c):
         wait_halo(0, c)
-        derive(0, c)
-
-        def body(p, carry):
-            for q in range(4):
-                part, lap, advect = spatial(0, c, p, q)
-                d = dbuf[c, p, part]
-                value = omega * d - VISCOSITY * lap + advect
-                fld[1, 1 + p, c, part] = value
-                acc[0] += value * d
-            return carry
-
-        lax.fori_loop(0, 2, body, 0)
-
-    def prepare(c):
+
+        def body(p, q):
+            part, value = outer(0, c, p, q, -VISCOSITY)
+            value = fld[1, 1 + p, c, part] + value
+            fld[1, 1 + p, c, part] = value
+            acc[0] += value * dbuf[c, p, part]
+
+        tiles(body)
+
+    def prepare_inner(c):
+        derive(2, c)
+
+        def body(p, q):
+            part, value = inner(2, c, p, q, -VISCOSITY)
+            fld[3, 1 + p, c, part] = value
+
+        tiles(body)
+
+    def prepare_outer(c):
         wait_halo(2, c)
-        derive(2, c)
-
-        def body(p, carry):
-            for q in range(4):
-                part, lap, advect = spatial(2, c, p, q)
-                fld[3, 1 + p, c, part] = advect - VISCOSITY * lap
-            return carry
-
-        lax.fori_loop(0, 2, body, 0)
+
+        def body(p, q):
+            part, value = outer(2, c, p, q, -VISCOSITY)
+            fld[3, 1 + p, c, part] += value
+
+        tiles(body)
 
     def complete(c, omega):
-        def body(p, carry):
-            for q in range(4):
-                part = pl.ds(q * 32, 32)
-                d = dbuf[c, p, part]
-                value = omega * d + fld[3, 1 + p, c, part]
-                fld[3, 1 + p, c, part] = value
-                acc[1] += value * d
-            return carry
-
-        lax.fori_loop(0, 2, body, 0)
+        def body(p, q):
+            part = pl.ds(q * 32, 32)
+            d = dbuf[c, p, part]
+            value = omega * d + fld[3, 1 + p, c, part]
+            fld[3, 1 + p, c, part] = value
+            acc[1] += value * d
+
+        tiles(body)
         send_halo(3, c)
 
-    def descend(k, c, omega, store):
+    def field_inner(k, c, omega):
+        derive(k, c)
+
+        def body(p, q):
+            part, value = inner(k, c, p, q, VISCOSITY)
+            dbuf[c, p, part] = omega * dbuf[c, p, part] + value
+
+        tiles(body)
+
+    def field_outer(k, c, store):
         wait_halo(k, c)
-        derive(k, c)
-
-        def body(p, carry):
-            for q in range(4):
-                part, lap, advect = spatial(k, c, p, q)
-                rate = omega * dbuf[c, p, part] + VISCOSITY * lap + advect
-                store(p, part, fld[k - 1, 1 + p, c, part] + DESCENT * rate)
-            return carry
-
-        lax.fori_loop(0, 2, body, 0)
-
-    def next_field(c, omega):
+
+        def body(p, q):
+            part, value = outer(k, c, p, q, VISCOSITY)
+            rate = dbuf[c, p, part] + value
+            store(p, part, fld[k - 1, 1 + p, c, part] + DESCENT * rate)
+
+        tiles(body)
+
+    def next_outer(c):
         def store(p, part, value):
             fld[2, 1 + p, c, part] = value
 
-        descend(1, c, omega, store)
+        field_outer(1, c, store)
         send_halo(2, c)
 
     stages = (
-        (0, 8, z * 2 + core, lambda r: device(x, y, r // 2, r % 2)),
-        (8, 16, x * 4 + y, lambda r: device(r // 4, r % 4, z, core)),
+        (0, 16, y * 4 + z, lambda r: device(x, r // 4, r % 4, core)),
+        (16, 8, x * 2 + core, lambda r: device(r // 2, y, z, r % 2)),
     )
 
     def drift_send(it, stage, tile):
@@ -393,30 +415,36 @@
     omega = freq[0]
     for c in range(3):
         symmetrize(c)
+        residual_inner(c, omega)
     for c in range(3):
-        residual(c, omega)
+        residual_outer(c)
         if c == 2:
             drift_start(0)
         send_halo(1, c)
-    next_field(0, omega)
+    for c in range(3):
+        field_inner(1, c, omega)
+    next_outer(0)
     drift_send(0, 1, drift_sum(0, 0))
-    next_field(1, omega)
-    next_field(2, omega)
-    prepare(0)
+    prepare_inner(0)
+    next_outer(1)
+    next_outer(2)
+    prepare_outer(0)
     omega = drift_end(0, omega)
     for c in range(3):
         if c > 0:
-            prepare(c)
+            prepare_inner(c)
+            prepare_outer(c)
         complete(c, omega)
         if c == 2:
             drift_start(1)
         send_out(0, c, lambda p: fld.at[3, 1 + p, c])
     for c in range(3):
+        field_inner(3, c, omega)
 
         def keep(p, part, value):
             orb[p, part] = value
 
-        descend(3, c, omega, keep)
+        field_outer(3, c, keep)
         if c == 0:
             drift_send(1, 1, drift_sum(1, 0))
         send_out(1, c, lambda p: orb.at[p])

time: 88.6 us -> 86.5 us (0.976)
  Pallas kernels: 87.2 us -> 85.1 us
    pallas_call x1, Pallas kernels: 84.9 us -> 82.8 us  [shards(): pl.pallas_call(kernel, out_shape=(pltpu.VMEM(cut, F32), pltpu.VMEM(cut, F...]
where the time goes in v4:
time: 86.5 us; the launch traced here: 86.4 us
  Pallas kernels  85.1 us (98%)
  between operations  1.28 us (1%)
    pallas_call x1, Pallas kernels, shards(): pl.pallas_call(kernel, out_shape=(pltpu.VMEM(cut, F32), pltpu.VMEM(cut, F...  82.8 us
    pallas_call x1, Pallas kernels, shards(): pl.pallas_call(finish, out_shape=shapes, in_specs=[vmem, vmem, hbm], out_...  2.35 us

profile of v4, /device:TPU:1, one launch (start us, length us, event | category | flops | bytes accessed | tf_op | source)
XLA Modules:
  0.0 86.4 jit_solution(14333252347721905098)
XLA Ops:
  1.3 82.8 %shard_map.67 = (f32[2,3,2,16,8,256]{5,4,3,2,1,0:T(8,128)S(1)}, f32[2,3,2,16,8,256]{5,4,3,2,1,0:T(8,128)S(1)}, f32[1]{0:T(128)}) custom-call(f32[1]{0:T(128)S(6)} %copy.9.freq_in, s32[16]{0:T(128)} %times_in.1, s32[1,256]{1,0:T(1,128)} %bitcast.9, f32[2,3,2,16,8,256]{5,4,3,2,1,0:T(8,128)} %bitcast.8), custom_call_target="tpu_custom_call" | custom-call | tf_op jit(solution)/shard_map/pallas_call | solution.py:509
  84.1 2.4 %shard_map.68 = (f32[2,3,2,16,8,256]{5,4,3,2,1,0:T(8,128)}, f32[2,3,2,16,8,256]{5,4,3,2,1,0:T(8,128)}, f32[1]{0:T(128)}) custom-call(f32[2,3,2,16,8,256]{5,4,3,2,1,0:T(8,128)S(1)} %get-tuple-element.9.orbit, f32[2,3,2,16,8,256]{5,4,3,2,1,0:T(8,128)S(1)} %get-tuple-element.10.defect, f32[1]{0:T(128)} %get-tuple-element.11.new), custom_call_target="tpu_custom_call" | custom-call | tf_op jit(solution)/shard_map/pallas_call | solution.py:552

commit v5 on v4

--- a/solution.py
+++ b/solution.py
@@ -390,7 +390,7 @@
             lax.fori_loop(0, 8, build, 0)
 
             def body(k, carry):
-                di = (inst + k) % 8
+                di = (inst + 1 + k) % 8
                 ds = x * 4 + core * 2 + p
                 src = obuf.at[o, c, p * 8 + di]
                 dst = outs[o].at[:, c, :, myj]
@@ -429,14 +429,15 @@
     next_outer(1)
     next_outer(2)
     prepare_outer(0)
+    prepare_inner(1)
+    prepare_inner(2)
     omega = drift_end(0, omega)
     for c in range(3):
         if c > 0:
-            prepare_inner(c)
             prepare_outer(c)
         complete(c, omega)
-        if c == 2:
-            drift_start(1)
+    drift_start(1)
+    for c in range(3):
         send_out(0, c, lambda p: fld.at[3, 1 + p, c])
     for c in range(3):
         field_inner(3, c, omega)
@@ -445,9 +446,8 @@
             orb[p, part] = value
 
         field_outer(3, c, keep)
-        if c == 0:
-            drift_send(1, 1, drift_sum(1, 0))
         send_out(1, c, lambda p: orb.at[p])
+    drift_send(1, 1, drift_sum(1, 0))
     freq[0] = drift_end(1, omega)
     result = pltpu.make_async_copy(freq, fout, small.at[0])
     result.start()

time: 86.5 us -> 85.6 us (0.990)
  Pallas kernels: 85.1 us -> 84.2 us
    pallas_call x1, Pallas kernels: 82.8 us -> 81.8 us  [shards(): pl.pallas_call(kernel, out_shape=(pltpu.VMEM(cut, F32), pltpu.VMEM(cut, F...]
where the time goes in v5:
time: 85.6 us; the launch traced here: 85.5 us
  Pallas kernels  84.2 us (98%)
  between operations  1.28 us (1%)
    pallas_call x1, Pallas kernels, shards(): pl.pallas_call(kernel, out_shape=(pltpu.VMEM(cut, F32), pltpu.VMEM(cut, F...  81.8 us
    pallas_call x1, Pallas kernels, shards(): pl.pallas_call(finish, out_shape=shapes, in_specs=[vmem, vmem, hbm], out_...  2.35 us

profile of v5, /device:TPU:1, one launch (start us, length us, event | category | flops | bytes accessed | tf_op | source)
XLA Modules:
  0.0 85.5 jit_solution(7846755282663718862)
XLA Ops:
  1.3 81.8 %shard_map.67 = (f32[2,3,2,16,8,256]{5,4,3,2,1,0:T(8,128)S(1)}, f32[2,3,2,16,8,256]{5,4,3,2,1,0:T(8,128)S(1)}, f32[1]{0:T(128)}) custom-call(f32[1]{0:T(128)S(6)} %copy.9.freq_in, s32[16]{0:T(128)} %times_in.1, s32[1,256]{1,0:T(1,128)} %bitcast.9, f32[2,3,2,16,8,256]{5,4,3,2,1,0:T(8,128)} %bitcast.8), custom_call_target="tpu_custom_call" | custom-call | tf_op jit(solution)/shard_map/pallas_call | solution.py:509
  83.1 2.4 %shard_map.68 = (f32[2,3,2,16,8,256]{5,4,3,2,1,0:T(8,128)}, f32[2,3,2,16,8,256]{5,4,3,2,1,0:T(8,128)}, f32[1]{0:T(128)}) custom-call(f32[2,3,2,16,8,256]{5,4,3,2,1,0:T(8,128)S(1)} %get-tuple-element.9.orbit, f32[2,3,2,16,8,256]{5,4,3,2,1,0:T(8,128)S(1)} %get-tuple-element.10.defect, f32[1]{0:T(128)} %get-tuple-element.11.new), custom_call_target="tpu_custom_call" | custom-call | tf_op jit(solution)/shard_map/pallas_call | solution.py:552

commit v6 on v5

--- a/solution.py
+++ b/solution.py
@@ -336,23 +336,26 @@
         field_outer(1, c, store)
         send_halo(2, c)
 
+    def apart(*steps):
+        return -sum(min(d, 4 - d) for d in steps)
+
+    turns = [(a, b) for a in range(4) for b in range(4)][1:]
+    turns.sort(key=lambda d: apart(*d))
+    hops = [(a, b) for a in range(4) for b in range(2)][1:]
+    hops.sort(key=lambda d: apart(*d))
     stages = (
-        (0, 16, y * 4 + z, lambda r: device(x, r // 4, r % 4, core)),
-        (16, 8, x * 2 + core, lambda r: device(r // 2, y, z, r % 2)),
+        (0, 16, y * 4 + z, [device(x, (y + a) % 4, (z + b) % 4, core) for a, b in turns]),
+        (16, 8, x * 2 + core, [device((x + a) % 4, y, z, (core + b) % 2) for a, b in hops]),
     )
 
     def drift_send(it, stage, tile):
-        base, size, rank, of = stages[stage]
+        base, _, rank, partners = stages[stage]
         drift[it, base + rank] = tile
-
-        def body(k, carry):
+        for partner in partners:
             pltpu.make_async_remote_copy(
                 drift.at[it, base + rank], drift.at[it, base + rank], d_send,
-                d_recv.at[it, stage], device_id=of((rank + k) % size), device_id_type=MESH,
+                d_recv.at[it, stage], device_id=partner, device_id_type=MESH,
             ).start()
-            return carry
-
-        lax.fori_loop(1, size, body, 0)
 
     def drift_sum(it, stage):
         base, size, _, _ = stages[stage]

time: 85.6 us -> 85.3 us (level)
  no operation moved by 1% of the time
where the time goes in v6:
time: 85.3 us; the launch traced here: 85.2 us
  Pallas kernels  83.9 us (98%)
  between operations  1.28 us (2%)
    pallas_call x1, Pallas kernels, shards(): pl.pallas_call(kernel, out_shape=(pltpu.VMEM(cut, F32), pltpu.VMEM(cut, F...  81.5 us
    pallas_call x1, Pallas kernels, shards(): pl.pallas_call(finish, out_shape=shapes, in_specs=[vmem, vmem, hbm], out_...  2.35 us

profile of v6, /device:TPU:1, one launch (start us, length us, event | category | flops | bytes accessed | tf_op | source)
XLA Modules:
  0.0 85.2 jit_solution(11255266062574834018)
XLA Ops:
  1.3 81.5 %shard_map.67 = (f32[2,3,2,16,8,256]{5,4,3,2,1,0:T(8,128)S(1)}, f32[2,3,2,16,8,256]{5,4,3,2,1,0:T(8,128)S(1)}, f32[1]{0:T(128)}) custom-call(f32[1]{0:T(128)S(6)} %copy.9.freq_in, s32[16]{0:T(128)} %times_in.1, s32[1,256]{1,0:T(1,128)} %bitcast.9, f32[2,3,2,16,8,256]{5,4,3,2,1,0:T(8,128)} %bitcast.8), custom_call_target="tpu_custom_call" | custom-call | tf_op jit(solution)/shard_map/pallas_call | solution.py:512
  82.8 2.4 %shard_map.68 = (f32[2,3,2,16,8,256]{5,4,3,2,1,0:T(8,128)}, f32[2,3,2,16,8,256]{5,4,3,2,1,0:T(8,128)}, f32[1]{0:T(128)}) custom-call(f32[2,3,2,16,8,256]{5,4,3,2,1,0:T(8,128)S(1)} %get-tuple-element.9.orbit, f32[2,3,2,16,8,256]{5,4,3,2,1,0:T(8,128)S(1)} %get-tuple-element.10.defect, f32[1]{0:T(128)} %get-tuple-element.11.new), custom_call_target="tpu_custom_call" | custom-call | tf_op jit(solution)/shard_map/pallas_call | solution.py:555

commit v7 on v5

--- a/solution.py
+++ b/solution.py
@@ -148,7 +148,7 @@
     left = chip_of((myj + 15) % 16)
     right = chip_of((myj + 1) % 16)
 
-    def send_halo(k, c):
+    def send_planes(k, c, p):
         def planes(up, target):
             src, dst = (2, 0) if up else (1, 3)
             pltpu.make_async_remote_copy(
@@ -156,22 +156,20 @@
                 y_recv.at[k, int(up), c], device_id=target, device_id_type=MESH,
             ).start()
 
-        @pl.when(core == 0)
+        @pl.when(core == 1 - p)
         def _():
-            planes(True, near)
-
-        @pl.when(core == 1)
+            planes(p == 1, near)
+
+        @pl.when((core == p) & (x < 3 if p == 1 else x > 0))
         def _():
-            planes(False, near)
-
-        @pl.when((core == 1) & (x < 3))
-        def _():
-            planes(True, far)
-
-        @pl.when((core == 0) & (x > 0))
-        def _():
-            planes(False, far)
-
+            planes(p == 1, far)
+
+    def send_halo(k, c):
+        for p in range(2):
+            send_planes(k, c, p)
+        send_rows(k, c)
+
+    def send_rows(k, c):
         for p in range(2):
             part = pl.ds(16 * p, 16)
             tiles = fld[k, 1 + p, c].reshape(16, 8, 256)
@@ -227,20 +225,27 @@
 
     def outer(k, c, p, q, scale):
         part = pl.ds(q * 32, 32)
-        edge = pl.ds(pl.multiple_of(16 * p, 16), 16)
+        start = 16 * p
+        edge = pl.ds(start if isinstance(p, int) else pl.multiple_of(start, 16), 16)
         half = 0.5 * speed_of(p)
         before = spread((scale - half) * xrecv[k, 0, c, edge][q * 4 : q * 4 + 4])
         after = spread((scale + half) * xrecv[k, 1, c, edge][q * 4 : q * 4 + 4])
         rows = jnp.where(row == 0, before, jnp.where(row == 7, after, 0.0))
         return part, scale * fld[k, 3 * p, c, part] + rows
 
-    def tiles(body):
+    def tiles(body, after=None):
         def step(p, carry):
             for q in range(4):
                 body(p, q)
+            if after is not None:
+                after(p)
             return carry
 
-        lax.fori_loop(0, 2, step, 0)
+        if after is None:
+            lax.fori_loop(0, 2, step, 0)
+        else:
+            for p in range(2):
+                step(p, 0)
 
     def derive(k, c):
         for p in range(2):
@@ -259,7 +264,8 @@
             other = jnp.concatenate([take(p, t + 8, 1) for t in range(16)], axis=0)
             own = jnp.concatenate([take(p, t, 0) for t in range(16)], axis=0)
             fld[0, 1 + p, c] = 0.5 * (own + signed(c, reflect_z(other)))
-        send_halo(0, c)
+            send_planes(0, c, p)
+        send_rows(0, c)
 
     def residual_inner(c, omega):
         derive(0, c)
@@ -319,7 +325,7 @@
 
         tiles(body)
 
-    def field_outer(k, c, store):
+    def field_outer(k, c, store, after=None):
         wait_halo(k, c)
 
         def body(p, q):
@@ -327,14 +333,14 @@
             rate = dbuf[c, p, part] + value
             store(p, part, fld[k - 1, 1 + p, c, part] + DESCENT * rate)
 
-        tiles(body)
+        tiles(body, after)
 
     def next_outer(c):
         def store(p, part, value):
             fld[2, 1 + p, c, part] = value
 
-        field_outer(1, c, store)
-        send_halo(2, c)
+        field_outer(1, c, store, lambda p: send_planes(2, c, p))
+        send_rows(2, c)
 
     stages = (
         (0, 16, y * 4 + z, lambda r: device(x, r // 4, r % 4, core)),

time: 85.6 us -> 85.7 us (level)
  no operation moved by 1% of the time
where the time goes in v7:
time: 85.7 us; the launch traced here: 85.6 us
  Pallas kernels  84.3 us (98%)
  between operations  1.28 us (1%)
    pallas_call x1, Pallas kernels, shards(): pl.pallas_call(kernel, out_shape=(pltpu.VMEM(cut, F32), pltpu.VMEM(cut, F...  82 us
    pallas_call x1, Pallas kernels, shards(): pl.pallas_call(finish, out_shape=shapes, in_specs=[vmem, vmem, hbm], out_...  2.35 us

profile of v7, /device:TPU:1, one launch (start us, length us, event | category | flops | bytes accessed | tf_op | source)
XLA Modules:
  0.0 85.6 jit_solution(8861045856488300324)
XLA Ops:
  1.3 82.0 %shard_map.67 = (f32[2,3,2,16,8,256]{5,4,3,2,1,0:T(8,128)S(1)}, f32[2,3,2,16,8,256]{5,4,3,2,1,0:T(8,128)S(1)}, f32[1]{0:T(128)}) custom-call(f32[1]{0:T(128)S(6)} %copy.9.freq_in, s32[16]{0:T(128)} %times_in.1, s32[1,256]{1,0:T(1,128)} %bitcast.9, f32[2,3,2,16,8,256]{5,4,3,2,1,0:T(8,128)} %bitcast.8), custom_call_target="tpu_custom_call" | custom-call | tf_op jit(solution)/shard_map/pallas_call | solution.py:515
  83.3 2.4 %shard_map.68 = (f32[2,3,2,16,8,256]{5,4,3,2,1,0:T(8,128)}, f32[2,3,2,16,8,256]{5,4,3,2,1,0:T(8,128)}, f32[1]{0:T(128)}) custom-call(f32[2,3,2,16,8,256]{5,4,3,2,1,0:T(8,128)S(1)} %get-tuple-element.9.orbit, f32[2,3,2,16,8,256]{5,4,3,2,1,0:T(8,128)S(1)} %get-tuple-element.10.defect, f32[1]{0:T(128)} %get-tuple-element.11.new), custom_call_target="tpu_custom_call" | custom-call | tf_op jit(solution)/shard_map/pallas_call | solution.py:558
